TPU v7x, 512 devices: a whole 4x8x8 slice. The times are simulated.
512 devices in a mesh: dp: 2 (over y_hi), seq: 32 (over y_lo, x, core), expert: 8 (over z).
Axes of the slice: x: 4, y: 8 (y_hi: 2, y_lo: 4; y = y_hi * 4 + y_lo), z: 8, core: 2. Of those that a mesh axis runs over, the one named last changes fastest.
Arguments:
- tokens: bfloat16 [2, 24576, 1280], P('dp', 'seq'), may hold values from -36 to 36
- slot_weight: bfloat16 [1024, 1280], P(('seq', 'expert')), may hold values from -1.5 to 1.5
- slot_output: bfloat16 [2, 1024, 1280], P('dp', ('seq', 'expert')), may hold values from -6 to 6
- slot_input_grad: bfloat16 [2, 1024, 1280], P('dp', ('seq', 'expert')), may hold values from -0.59765625 to 0.59765625
- output_grad: bfloat16 [2, 24576, 1280], P('dp', 'seq'), may hold values from -1.1953125 to 1.1953125
Outputs:
- token_grad: bfloat16 [2, 24576, 1280], P('dp', ('seq', 'expert'))
- slot_output_grad: bfloat16 [2, 1024, 1280], P('dp', ('seq', 'expert'))
- slot_weight_grad: float32 [1024, 1280], P(('seq', 'expert'))
All inputs are finite; a program needn't handle non-finite values.
Results may differ from a plain program's by a relative error of at most 0.015.
Values may be sent and summed in bfloat16 or wider, within the bound.
A program may use at most 64 MiB of HBM per device.

v0:
```python
import jax
import jax.numpy as jnp
from jax import lax
from jax.sharding import PartitionSpec as P


def on_device(tokens, slot_weight, slot_output, slot_input_grad, output_grad):
    token_rows = tokens[0]
    grad_rows = output_grad[0]
    phi_local, outputs_local, inputs_local = (
        lax.all_gather(slot_weight, "seq", axis=0, tiled=True),
        lax.all_gather(slot_output[0], "seq", axis=0, tiled=True),
        lax.all_gather(slot_input_grad[0], "seq", axis=0, tiled=True),
    )
    logits = jnp.einsum("td,ed->te", token_rows, phi_local, preferred_element_type=jnp.float32)
    column_peak = lax.pmax(jnp.max(logits, axis=0), "seq")
    column_exp = jnp.exp(logits - column_peak[None, :])
    column_mass = lax.psum(jnp.sum(column_exp, axis=0), "seq")
    dispatch = column_exp / column_mass[None, :]
    row_peak = lax.pmax(jnp.max(logits, axis=1), "expert")
    row_exp = jnp.exp(logits - row_peak[:, None])
    row_mass = lax.psum(jnp.sum(row_exp, axis=1), "expert")
    combine = row_exp / row_mass[:, None]
    combine_grad = jnp.einsum(
        "td,ed->te", grad_rows, outputs_local, preferred_element_type=jnp.float32
    )
    dispatch_grad = jnp.einsum(
        "td,ed->te", token_rows, inputs_local, preferred_element_type=jnp.float32
    )
    row_dot = lax.psum(jnp.sum(combine * combine_grad, axis=1), "expert")
    column_dot = lax.psum(jnp.sum(dispatch * dispatch_grad, axis=0), "seq")
    logit_grad = combine * (combine_grad - row_dot[:, None]) + dispatch * (
        dispatch_grad - column_dot[None, :]
    )
    logit_half = logit_grad.astype(jnp.bfloat16)
    dispatch_half = dispatch.astype(jnp.bfloat16)
    combine_half = combine.astype(jnp.bfloat16)
    token_single = token_rows.astype(jnp.float32)
    output_term = jnp.einsum(
        "te,td->ed", combine_half, grad_rows, preferred_element_type=jnp.float32
    )
    weight_term = jnp.einsum(
        "te,td->ed",
        logit_grad,
        token_single,
        precision=lax.Precision.HIGHEST,
        preferred_element_type=jnp.float32,
    )
    slot_sums = lax.psum_scatter(
        jnp.stack([output_term, weight_term], axis=1), "seq", scatter_dimension=0, tiled=True
    )
    slot_output_grad = slot_sums[:, 0, :].astype(jnp.bfloat16)[None]
    slot_weight_grad = lax.psum(slot_sums[:, 1, :], "dp")
    factors = jnp.concatenate([dispatch_half, logit_half], axis=1)
    stacked = jnp.concatenate([inputs_local, phi_local], axis=0)
    token_total = lax.psum_scatter(
        jnp.dot(factors, stacked, preferred_element_type=jnp.float32).astype(jnp.bfloat16),
        "expert",
        scatter_dimension=0,
        tiled=True,
    )
    token_grad = token_total[None]
    return (token_grad, slot_output_grad, slot_weight_grad)


def solution(mesh):
    placed = (
        P("dp", "seq", None),
        P(("seq", "expert"), None),
        P("dp", ("seq", "expert"), None),
        P("dp", ("seq", "expert"), None),
        P("dp", "seq", None),
    )
    return jax.shard_map(
        on_device,
        mesh=mesh,
        in_specs=placed,
        out_specs=(
            P("dp", ("seq", "expert"), None),
            P("dp", ("seq", "expert"), None),
            P(("seq", "expert"), None),
        ),
        check_vma=False,
    )
```

profile of v0, /device:TPU:6, one launch (start us, length us, event | category | flops | bytes accessed | tf_op | source)
XLA Modules:
  0.0 692.4 jit_solution(15294157375065904264)
XLA Ops:
  8.0 0.0 copy-start
  8.0 0.0 all-reduce.3.cloned.1.call-start
  8.1 40.1 %all-gather.2 = bf16[32,4,1280]{2,1,0:T(4,128)(2,1)S(1)} all-gather(bf16[1,4,1280]{2,1,0:T(4,128)(2,1)} %bitcast.40), channel_id=1, replica_groups=mesh['dp'=2,'seq'=32,'expert'=8] {'seq'}, dimensions={0}, use_global_device_ids=true | all-gather | bytes 337920 | tf_op jit(solution)/shard_map/all_gather | solution.py:11
  48.2 0.1 reshape.26
  48.3 2.4 fusion.25
  50.7 18.5 %pmax.15 = f32[768]{0:T(1024)S(1)} all-reduce(f32[768]{0:T(1024)S(1)} %get-tuple-element.7), channel_id=1, replica_groups=mesh['dp'=2,'seq'=32,'expert'=8] {'expert'}, use_global_device_ids=true, to_apply=%region_5.0 | all-reduce | flops 768 | bytes 6144 | tf_op jit(solution)/shard_map/pmax | solution.py:20
  69.2 59.9 %pmax.14 = f32[128]{0:T(128)S(1)} all-reduce(f32[128]{0:T(128)S(1)} %get-tuple-element.8), channel_id=1, replica_groups=mesh['dp'=2,'seq'=32,'expert'=8] {'seq'}, use_global_device_ids=true, to_apply=%region_1.0 | all-reduce | flops 128 | bytes 1024 | tf_op jit(solution)/shard_map/pmax | solution.py:16
  129.1 0.2 fusion.17
  129.3 14.2 %psum.36 = f32[768]{0:T(1024)S(1)} all-reduce(f32[768]{0:T(1024)S(1)} %get-tuple-element.5), channel_id=1, replica_groups=mesh['dp'=2,'seq'=32,'expert'=8] {'expert'}, use_global_device_ids=true, to_apply=%region_7.0 | all-reduce | flops 768 | bytes 6144 | tf_op jit(solution)/shard_map/psum | solution.py:22
  143.5 67.4 %psum.35 = f32[128]{0:T(128)S(1)} all-reduce(f32[128]{0:T(128)S(1)} %get-tuple-element.6), channel_id=1, replica_groups=mesh['dp'=2,'seq'=32,'expert'=8] {'seq'}, use_global_device_ids=true, to_apply=%region_3.0 | all-reduce | flops 128 | bytes 1024 | tf_op jit(solution)/shard_map/psum | solution.py:18
  210.9 0.0 copy-done.3
  210.9 51.9 %all-gather.1 = bf16[1,128,1280]{2,0,1:T(2,128)(2,1)S(1)} all-gather(bf16[1,4,1280]{2,0,1:T(2,128)(2,1)S(1)} %copy.15), channel_id=3, replica_groups=mesh['dp'=2,'seq'=32,'expert'=8] {'seq'}, dimensions={1}, use_global_device_ids=true | all-gather | bytes 337920 | tf_op jit(solution)/shard_map/all_gather | solution.py:13
  262.8 2.3 fusion.4
  265.2 0.0 copy-done.4
  265.2 39.4 %all-gather = bf16[1,128,1280]{2,0,1:T(2,128)(2,1)S(1)} all-gather(bf16[1,4,1280]{2,0,1:T(2,128)(2,1)S(1)} %copy.14), channel_id=2, replica_groups=mesh['dp'=2,'seq'=32,'expert'=8] {'seq'}, dimensions={1}, use_global_device_ids=true | all-gather | bytes 337920 | tf_op jit(solution)/shard_map/all_gather | solution.py:12
  304.6 1.3 convolution_bitcast_fusion.1
  305.8 1.6 multiply_reduce_fusion.1
  307.4 16.1 %psum.37 = f32[768]{0:T(1024)S(1)} all-reduce(f32[768]{0:T(1024)S(1)} %get-tuple-element.3), channel_id=1, replica_groups=mesh['dp'=2,'seq'=32,'expert'=8] {'expert'}, use_global_device_ids=true, to_apply=%region_9.0 | all-reduce | flops 768 | bytes 6144 | tf_op jit(solution)/shard_map/psum | solution.py:30
  323.5 56.8 %psum.38 = f32[128]{0:T(128)S(1)} all-reduce(f32[128]{0:T(128)S(1)} %get-tuple-element.4), channel_id=1, replica_groups=mesh['dp'=2,'seq'=32,'expert'=8] {'seq'}, use_global_device_ids=true, to_apply=%region_11.0 | all-reduce | flops 128 | bytes 1024 | tf_op jit(solution)/shard_map/psum | solution.py:31
  380.3 2.0 fusion.26
  382.3 2.5 convolution_bitcast_fusion
  384.8 0.0 copy-start.5
  384.8 1.1 pad_maximum_fusion
  386.0 0.0 all-reduce.3.cloned.1.call-update
  386.0 0.0 reduce-scatter.3.cloned.1.call-start
  386.1 2.0 convolution_convert_fusion
  388.1 0.0 reduce-scatter.3.cloned.1.call-update
  388.1 1.3 dynamic-slice
  390.0 278.8 %all-reduce.3.cloned.1.call-done = f32[128,2,1280]{2,0,1:T(8,128)} async-done(((f32[128,2,1280]{2,0,1:T(8,128)}), f32[128,2,1280]{2,0,1:T(8,128)}) %all-reduce.3.cloned.1.call-update) | async-done | bytes 1310736
  668.8 0.8 dynamic-slice_bitcast_fusion
  669.6 14.0 %psum.39 = f32[4,1280]{1,0:T(4,128)} all-reduce(f32[4,1280]{1,0:T(4,128)S(1)} %dynamic-slice_bitcast_fusion), channel_id=1, replica_groups=mesh['dp'=2,'seq'=32,'expert'=8] {'dp'}, use_global_device_ids=true, to_apply=%region_14.0 | all-reduce | flops 5120 | bytes 40960 | tf_op jit(solution)/shard_map/psum | solution.py:53
  683.6 1.4 fusion.21
  (12 shorter events, 0.1 us)
Async XLA Ops:
  8.0 296.6 %copy-start = (bf16[1,768,1280]{2,1,0:T(8,128)(2,1)S(1)}, bf16[1,768,1280]{2,1,0:T(8,128)(2,1)}, u32[]{:S(2)}) copy-start(bf16[1,768,1280]{2,1,0:T(8,128)(2,1)} %param.9) | copy-start | bytes 5898244
  8.0 660.8 %all-reduce.3.cloned.1.call-start = ((), (), s32[]{:S(2)}) async-start(), calls=%async_computation.2 | async-start | bytes 2621440
  48.2 162.7 %copy-start.3 = (bf16[1,4,1280]{2,1,0:T(4,128)(2,1)S(1)}, bf16[1,4,1280]{2,1,0:T(4,128)(2,1)}, u32[]{:S(2)}) copy-start(bf16[1,4,1280]{2,1,0:T(4,128)(2,1)} %param.8) | copy-start | bytes 30724
  262.8 2.4 copy-start.4
  380.3 4.5 copy-start.1
  384.8 1.2 copy-start.2
  384.8 1.2 copy-start.5
  386.0 299.0 %reduce-scatter.3.cloned.1.call-start = ((), (), s32[]{:S(2)}) async-start(), calls=%async_computation.1 | async-start | bytes 2211840 | tf_op jit(solution)/shard_map/reduce_scatter | solution.py:56
Sparse Core Ops, SparseCore 0:
  386.1 282.6 all-reduce.2
Sparse Core Ops, SparseCore 1:
  389.9 54.5 reduce-scatter.2
where the time goes:
time: 706 us; the launch traced here: 692 us
  blocking collectives  378 us (54%)
  waiting for transfers between devices  279 us (40%)
  between operations  16.2 us (2%)
  matrix products  12.1 us (2%)
    unnamed x3, waiting for transfers between devices  279 us
    psum x1, blocking collectives, on_device(): column_mass = lax.psum(jnp.sum(column_exp, axis=0), 'seq')  67.4 us
    pmax x1, blocking collectives, on_device(): column_peak = lax.pmax(jnp.max(logits, axis=0), 'seq')  59.9 us
    psum x1, blocking collectives, on_device(): column_dot = lax.psum(jnp.sum(dispatch * dispatch_grad, axis=0), 'seq')  56.8 us
    all_gather x1, blocking collectives, on_device(): lax.all_gather(slot_input_grad[0], 'seq', axis=0, tiled=True)  51.9 us
    all_gather x1, blocking collectives, on_device(): lax.all_gather(slot_weight, 'seq', axis=0, tiled=True)  40.1 us
    all_gather x1, blocking collectives, on_device(): lax.all_gather(slot_output[0], 'seq', axis=0, tiled=True)  39.4 us
    pmax x1, blocking collectives, on_device(): row_peak = lax.pmax(jnp.max(logits, axis=1), 'expert')  18.5 us
  transfers between devices with their start and end apart: 2, of which 1 were waited for; matrix products, arithmetic and copies ran while one was open for 1% of the time, Pallas kernels for 0%

commit v1 on v0

v1 whole, which is shorter than its diff:
```python
import jax
import jax.numpy as jnp
from jax import lax
from jax.experimental import pallas as pl
from jax.experimental.pallas import tpu as pltpu
from jax.sharding import PartitionSpec as P

F32 = jnp.float32
BF16 = jnp.bfloat16
MESH = pl.DeviceIdType.MESH

NY, NX, NC, NZ = 4, 4, 2, 8
NSEQ = NY * NX * NC
D = 1280
TOK = 768
EXP = 128
OWN = TOK // NZ
HALF = OWN // 2

RIGHT = ((4, 0), (3, 1), (3, 0), (2, 1), (2, 0), (1, 1), (1, 0))
LEFT = ((4, 1), (3, 0), (3, 1), (2, 0), (2, 1), (1, 0), (1, 1))


def nt_dot(a, b):
    return lax.dot_general(a, b, (((1,), (1,)), ((), ())), preferred_element_type=F32)


def nn_dot(a, b):
    return jnp.dot(a, b, preferred_element_type=F32)


def kernel(
    tok_hbm, phi_ref, out_ref, inp_ref, og_hbm,
    tg_ref, so_ref, sw_ref,
    tok, og, shard, params, logit, cgrad, dgrad, row_exp, col_exp, col_tile, row_stat, col_stat,
    mat, comb, fac, part, stage, ring_in,
    w_sum, o_sum, w_core, o_core, w_x, o_x, w_xin, o_xin, y_out, y_in, dp_out, dp_in,
    load_sem, ys, yr, xs, xr, cs, cr, stat_s, stat_r, ring_s, ring_r, rc_s, rc_r, rx_s, rx_r, ry_s, ry_r, dp_s, dp_r,
):
    dp = lax.axis_index("dp")
    seq = lax.axis_index("seq")
    z = lax.axis_index("expert")
    core = lax.rem(seq, NC)
    x = lax.rem(seq // NC, NX)
    y = seq // (NC * NX)

    def seq_of(yy, xx, cc):
        return (yy * NX + xx) * NC + cc

    load_tok = pltpu.make_async_copy(tok_hbm, tok, load_sem.at[0])
    load_og = pltpu.make_async_copy(og_hbm, og, load_sem.at[1])
    load_tok.start()
    load_og.start()
    shard[y, 0] = phi_ref[...]
    shard[y, 1] = inp_ref[...]
    shard[y, 2] = out_ref[...]

    barrier = pltpu.get_barrier_semaphore()

    @pl.loop(1, NSEQ)
    def _(j):
        pl.semaphore_signal(
            barrier, inc=1, device_id={"seq": lax.rem(seq + j, NSEQ)}, device_id_type=MESH
        )

    @pl.loop(1, NZ)
    def _(j):
        pl.semaphore_signal(
            barrier, inc=1, device_id={"expert": lax.rem(z + j, NZ)}, device_id_type=MESH
        )

    pl.semaphore_signal(barrier, inc=1, device_id={"dp": 1 - dp}, device_id_type=MESH)
    pl.semaphore_wait(barrier, NSEQ + NZ - 1)

    pending = []

    def send(src, dst, s_sem, r_sem, device):
        copy = pltpu.make_async_remote_copy(
            src_ref=src, dst_ref=dst, send_sem=s_sem, recv_sem=r_sem,
            device_id=device, device_id_type=MESH,
        )
        copy.start()
        pending.append(copy)
        return copy

    y_copies = [
        send(
            shard.at[y], shard.at[y], ys.at[j - 1], yr.at[j - 1],
            {"seq": seq_of(lax.rem(y + j, NY), x, core)},
        )
        for j in range(1, NY)
    ]
    for copy in y_copies:
        copy.wait_recv()
    for t in range(3):
        rows = [shard[j, t].astype(F32) for j in range(NY)]
        params[t, core, x] = jnp.concatenate(rows, axis=0).astype(BF16)
    sibling = {"seq": seq_of(y, x, 1 - core)}
    own_block = params.at[:, core, x]
    x_copies = [
        send(
            own_block, own_block, xs.at[j - 1], xr.at[j - 1],
            {"seq": seq_of(y, lax.rem(x + j, NX), core)},
        )
        for j in range(1, NX)
    ]
    c_copies = [send(own_block, own_block, cs.at[0], cr.at[0], sibling)]
    for j in (1, 3, 2):
        x_copies[j - 1].wait_recv()
        block = params.at[:, core, lax.rem(x - j + NX, NX)]
        c_copies.append(send(block, block, cs.at[j], cr.at[j], sibling))
    load_tok.wait()
    load_og.wait()
    for copy in c_copies:
        copy.wait_recv()

    both = params[0:2].reshape(2 * EXP, D)
    outs = params[2].reshape(EXP, D)
    for n in range(TOK // 256):
        cols = slice(256 * n, 256 * (n + 1))
        pair = nt_dot(both, tok[cols, :])
        logit[:, cols] = pair[:EXP]
        dgrad[:, cols] = pair[EXP:]
        cgrad[:, cols] = nt_dot(outs, og[cols, :])

    ROWS = 16
    blocks = [slice(ROWS * b, ROWS * (b + 1)) for b in range(EXP // ROWS)]
    top = logit[blocks[0], :]
    for rows in blocks[1:]:
        top = jnp.maximum(top, logit[rows, :])
    row_max = jnp.max(top, axis=0, keepdims=True)
    row_sum = jnp.zeros((ROWS, TOK), F32)
    row_dot = jnp.zeros((ROWS, TOK), F32)
    lane = lax.broadcasted_iota(jnp.int32, (ROWS, EXP), 1)
    for rows in blocks:
        value = logit[rows, :]
        by_row = jnp.exp(value - row_max)
        row_exp[rows, :] = by_row
        row_sum = row_sum + by_row
        row_dot = row_dot + by_row * cgrad[rows, :]
        col_max = jnp.max(value, axis=1, keepdims=True)
        by_col = jnp.exp(value - col_max)
        col_exp[rows, :] = by_col
        col_sum = jnp.sum(by_col, axis=1, keepdims=True)
        col_dot = jnp.sum(by_col * dgrad[rows, :], axis=1, keepdims=True)
        col_tile[rows, :] = jnp.where(
            lane == 0, col_max, jnp.where(lane == 1, col_sum, jnp.where(lane == 2, col_dot, 0.0))
        )
    row_stat[z] = jnp.concatenate(
        [
            row_max,
            jnp.sum(row_sum, axis=0, keepdims=True),
            jnp.sum(row_dot, axis=0, keepdims=True),
            jnp.zeros((1, TOK), F32),
        ],
        axis=0,
    )
    col_stat[seq] = col_tile[...].T[0:4, :]

    @pl.loop(1, NZ)
    def _(j):
        pltpu.make_async_remote_copy(
            src_ref=row_stat.at[z], dst_ref=row_stat.at[z],
            send_sem=stat_s.at[0], recv_sem=stat_r.at[0],
            device_id={"expert": lax.rem(z + j, NZ)}, device_id_type=MESH,
        ).start()

    @pl.loop(1, NSEQ)
    def _(j):
        pltpu.make_async_remote_copy(
            src_ref=col_stat.at[seq], dst_ref=col_stat.at[seq],
            send_sem=stat_s.at[1], recv_sem=stat_r.at[1],
            device_id={"seq": lax.rem(seq + j, NSEQ)}, device_id_type=MESH,
        ).start()

    row_all = row_stat.at[pl.ds(0, NZ - 1)]
    col_all = col_stat.at[pl.ds(0, NSEQ - 1)]
    pltpu.make_async_copy(row_all, row_all, stat_r.at[0]).wait()

    def join(stat, count):
        best = stat[0][0:1]
        for j in range(1, count):
            best = jnp.maximum(best, stat[j][0:1])
        total = jnp.zeros(stat.shape[1:], F32)
        for j in range(count):
            one = stat[j]
            total = total + jnp.exp(one[0:1] - best) * one
        return best, total[1:2], total[2:3]

    best, mass, dot = join(row_stat, NZ)
    row_scale = jnp.exp(row_stat[z][0:1] - best) / mass
    row_mean = dot / mass
    pltpu.make_async_copy(col_all, col_all, stat_r.at[1]).wait()
    best, mass, dot = join(col_stat, NSEQ)
    lines = lax.broadcasted_iota(jnp.int32, (EXP, EXP), 0)
    col_tile[...] = jnp.where(
        lines == 0,
        jnp.exp(col_stat[seq][0:1] - best) / mass,
        jnp.where(lines == 1, dot / mass, 0.0),
    ).T

    for b, rows in enumerate(blocks):
        combine = row_exp[rows, :] * row_scale
        dispatch = col_exp[rows, :] * col_tile[rows, 0:1]
        grad = combine * (cgrad[rows, :] - row_mean) + dispatch * (dgrad[rows, :] - col_tile[rows, 1:2])
        high = grad.astype(BF16)
        mat[rows, :] = (grad - high.astype(F32)).astype(BF16)
        mat[EXP + ROWS * b:EXP + ROWS * (b + 1), :] = high
        mat[2 * EXP + ROWS * b:2 * EXP + ROWS * (b + 1), :] = dispatch.astype(BF16)
        comb[rows, :] = combine.astype(BF16)
    fac[...] = mat[EXP:3 * EXP, :].T

    def term(d):
        stacked = params[0:2].reshape(2 * EXP, D)
        owner = lax.rem(z + d, NZ)
        part[d] = nn_dot(fac[pl.ds(pl.multiple_of(owner * OWN, OWN), OWN), :], stacked)

    ring = ({}, {})
    towards = ({"expert": lax.rem(z + 1, NZ)}, {"expert": lax.rem(z + NZ - 1, NZ)})

    def pass_on(way, i):
        d, h = (RIGHT, LEFT)[way][i]
        value = part[d if way == 0 else NZ - d, HALF * h:HALF * (h + 1), :]
        if (d + 1, h) in ring[way]:
            j, copy = ring[way][(d + 1, h)]
            copy.wait_recv()
            value = value + ring_in[way, j].astype(F32)
        stage[way, i] = value.astype(BF16)
        ring[way][(d, h)] = (
            i,
            send(stage.at[way, i], ring_in.at[way, i], ring_s.at[way, i], ring_r.at[way, i], towards[way]),
        )

    term(4)
    pass_on(0, 0)
    pass_on(1, 0)
    term(3)
    pass_on(0, 1)
    term(5)
    pass_on(1, 1)

    for n in range(D // 256):
        cols = slice(256 * n, 256 * (n + 1))
        pair = nn_dot(mat[0:2 * EXP, :], tok[:, cols])
        w_sum[:, cols] = pair[:EXP] + pair[EXP:]
        o_sum[:, cols] = nn_dot(comb[...], og[:, cols]).astype(BF16)
    there = pl.ds(pl.multiple_of((1 - core) * (EXP // 2), EXP // 2), EXP // 2)
    here = pl.ds(pl.multiple_of(core * (EXP // 2), EXP // 2), EXP // 2)
    core_w = send(w_sum.at[there], w_core, rc_s.at[0], rc_r.at[0], sibling)
    core_o = send(o_sum.at[there], o_core, rc_s.at[1], rc_r.at[1], sibling)
    for d in (2, 6, 1, 7, 0):
        term(d)

    pass_on(0, 2)
    pass_on(1, 2)

    core_w.wait_recv()
    core_o.wait_recv()
    w_x[...] = (w_sum[here, :] + w_core[...]).reshape(NX, 16, D)
    o_x[...] = (o_sum[here, :].astype(F32) + o_core[...].astype(F32)).astype(BF16).reshape(NX, 16, D)
    x_sums = []
    for j in range(1, NX):
        to = lax.rem(x + j, NX)
        device = {"seq": seq_of(y, to, core)}
        x_sums.append(send(w_x.at[to], w_xin.at[j - 1], rx_s.at[0, j - 1], rx_r.at[0, j - 1], device))
        x_sums.append(send(o_x.at[to], o_xin.at[j - 1], rx_s.at[1, j - 1], rx_r.at[1, j - 1], device))

    pass_on(0, 3)
    pass_on(1, 3)
    pass_on(0, 4)
    pass_on(1, 4)

    for copy in x_sums:
        copy.wait_recv()
    w16 = w_x[x]
    o16 = o_x[x].astype(F32)
    for j in range(NX - 1):
        w16 = w16 + w_xin[j]
        o16 = o16 + o_xin[j].astype(F32)
    for j in range(NY):
        y_out[j, 0:4] = w16[4 * j:4 * j + 4]
        y_out[j, 4:8] = o16[4 * j:4 * j + 4]
    y_sums = []
    for j in range(1, NY):
        to = lax.rem(y + j, NY)
        y_sums.append(
            send(y_out.at[to], y_in.at[j - 1], ry_s.at[j - 1], ry_r.at[j - 1], {"seq": seq_of(to, x, core)})
        )

    pass_on(0, 5)
    pass_on(1, 5)

    for copy in y_sums:
        copy.wait_recv()
    total = y_out[y]
    for j in range(NY - 1):
        total = total + y_in[j]
    dp_out[...] = total
    dp_copy = send(dp_out, dp_in, dp_s, dp_r, {"dp": 1 - dp})
    so_ref[...] = total[4:8].astype(BF16)

    pass_on(0, 6)
    pass_on(1, 6)

    dp_copy.wait_recv()
    sw_ref[...] = dp_out[0:4] + dp_in[0:4]

    for h in (1, 0):
        value = part[0, HALF * h:HALF * (h + 1), :]
        for way in range(2):
            j, copy = ring[way][(1, h)]
            copy.wait_recv()
            value = value + ring_in[way, j].astype(F32)
        tg_ref[HALF * h:HALF * (h + 1), :] = value.astype(BF16)

    for copy in pending:
        copy.wait_send()
    pltpu.make_async_copy(row_all, row_all, stat_s.at[0]).wait()
    pltpu.make_async_copy(col_all, col_all, stat_s.at[1]).wait()


def on_device(tokens, slot_weight, slot_output, slot_input_grad, output_grad):
    vmem = pl.BlockSpec(memory_space=pltpu.VMEM)
    hbm = pl.BlockSpec(memory_space=pl.ANY)
    dma = pltpu.SemaphoreType.DMA
    token_grad, slot_output_grad, slot_weight_grad = pl.pallas_call(
        kernel,
        out_shape=(
            jax.ShapeDtypeStruct((OWN, D), BF16),
            jax.ShapeDtypeStruct((4, D), BF16),
            jax.ShapeDtypeStruct((4, D), F32),
        ),
        in_specs=[hbm, vmem, vmem, vmem, hbm],
        out_specs=(vmem, vmem, vmem),
        scratch_shapes=[
            pltpu.VMEM((TOK, D), BF16),
            pltpu.VMEM((TOK, D), BF16),
            pltpu.VMEM((NY, 3, 4, D), BF16),
            pltpu.VMEM((3, NC, NX, 16, D), BF16),
            pltpu.VMEM((EXP, TOK), F32),
            pltpu.VMEM((EXP, TOK), F32),
            pltpu.VMEM((EXP, TOK), F32),
            pltpu.VMEM((EXP, TOK), F32),
            pltpu.VMEM((EXP, TOK), F32),
            pltpu.VMEM((EXP, EXP), F32),
            pltpu.VMEM((NZ, 4, TOK), F32),
            pltpu.VMEM((NSEQ, 4, EXP), F32),
            pltpu.VMEM((3 * EXP, TOK), BF16),
            pltpu.VMEM((EXP, TOK), BF16),
            pltpu.VMEM((TOK, 2 * EXP), BF16),
            pltpu.VMEM((NZ, OWN, D), F32),
            pltpu.VMEM((2, 7, HALF, D), BF16),
            pltpu.VMEM((2, 7, HALF, D), BF16),
            pltpu.VMEM((EXP, D), F32),
            pltpu.VMEM((EXP, D), BF16),
            pltpu.VMEM((EXP // 2, D), F32),
            pltpu.VMEM((EXP // 2, D), BF16),
            pltpu.VMEM((NX, 16, D), F32),
            pltpu.VMEM((NX, 16, D), BF16),
            pltpu.VMEM((NX - 1, 16, D), F32),
            pltpu.VMEM((NX - 1, 16, D), BF16),
            pltpu.VMEM((NY, 8, D), F32),
            pltpu.VMEM((NY - 1, 8, D), F32),
            pltpu.VMEM((8, D), F32),
            pltpu.VMEM((8, D), F32),
            dma((2,)),
            dma((3,)), dma((3,)),
            dma((3,)), dma((3,)),
            dma((4,)), dma((4,)),
            dma((2,)), dma((2,)),
            dma((2, 7)), dma((2, 7)),
            dma((2,)), dma((2,)),
            dma((2, 3)), dma((2, 3)),
            dma((3,)), dma((3,)),
            dma(()), dma(()),
        ],
        compiler_params=pltpu.CompilerParams(
            collective_id=0, has_side_effects=True, vmem_limit_bytes=50 * 1024 * 1024
        ),
        cost_estimate=pl.CostEstimate(
            flops=2_000_000_000, bytes_accessed=5_000_000, transcendentals=250_000
        ),
    )(tokens[0], slot_weight, slot_output[0], slot_input_grad[0], output_grad[0])
    return (token_grad[None], slot_output_grad[None], slot_weight_grad)


def solution(mesh):
    placed = (
        P("dp", "seq", None),
        P(("seq", "expert"), None),
        P("dp", ("seq", "expert"), None),
        P("dp", ("seq", "expert"), None),
        P("dp", "seq", None),
    )
    return jax.shard_map(
        on_device,
        mesh=mesh,
        in_specs=placed,
        out_specs=(
            P("dp", ("seq", "expert"), None),
            P("dp", ("seq", "expert"), None),
            P(("seq", "expert"), None),
        ),
        check_vma=False,
    )
```

time: 706 us -> 64.1 us (0.09); the launches traced: 692 us -> 63.2 us
  blocking collectives: 378 us -> 0 us
  waiting for transfers between devices: 279 us -> 0 us
  Pallas kernels: 0 us -> 57 us
  between operations: 16.2 us -> 0.65 us
  matrix products: 12.1 us -> 0 us
    unnamed x3 -> x0, waiting for transfers between devices: 279 us -> none
    psum x5 -> x0, blocking collectives: 168 us -> none  [the longest x1 67.4 us: on_device(): column_mass = lax.psum(jnp.sum(column_exp, axis=0), 'seq')]
    all_gather x3 -> x0, blocking collectives: 131 us -> none  [the longest x1 51.9 us: on_device(): lax.all_gather(slot_input_grad[0], 'seq', axis=0, tiled=True)]
    pmax x2 -> x0, blocking collectives: 78.4 us -> none  [the longest x1 59.9 us: on_device(): column_peak = lax.pmax(jnp.max(logits, axis=0), 'seq')]
    pallas_call x0 -> x1, Pallas kernels: none -> 57 us  [on_device(): pl.pallas_call(kernel, out_shape=(jax.ShapeDtypeStruct((OWN, D), BF16), j...]
    dot_general x6 -> x0, matrix products: 12.1 us -> none  [the longest x1 2.48 us: on_device(): jnp.einsum('te,td->ed', logit_grad, token_single, precision=lax.Precision...]
  transfers between devices with their start and end apart: 2 -> 0, of which waited for: 1 -> 0; matrix products, arithmetic and copies ran while one was open for 1% -> 0% of each run, Pallas kernels for 0% -> 0%
where the time goes in v1:
time: 64.1 us; the launch traced here: 63.2 us
  Pallas kernels  57 us (89%)
  local copies, waits for them, and re-layouts  5.54 us (9%)
  between operations  0.65 us (1%)
    pallas_call x1, Pallas kernels, on_device(): pl.pallas_call(kernel, out_shape=(jax.ShapeDtypeStruct((OWN, D), BF16), j...  57 us
    unnamed x11, local copies, waits for them, and re-layouts  5.54 us

profile of v1, /device:TPU:6, one launch (start us, length us, event | category | flops | bytes accessed | tf_op | source)
XLA Modules:
  0.0 63.2 jit_solution(15107737567404694760)
XLA Ops:
  0.6 0.0 copy-start
  0.6 1.5 %copy-done = bf16[1,768,1280]{2,1,0:T(8,128)(2,1)S(1)} copy-done((bf16[1,768,1280]{2,1,0:T(8,128)(2,1)S(1)}, bf16[1,768,1280]{2,1,0:T(8,128)(2,1)}, u32[]{:S(2)}) %copy-start) | copy-done | bytes 1966104
  2.2 0.0 copy-start.1
  2.2 0.7 %copy-done.1 = bf16[4,1280]{1,0:T(4,128)(2,1)S(1)} copy-done((bf16[4,1280]{1,0:T(4,128)(2,1)S(1)}, bf16[4,1280]{1,0:T(4,128)(2,1)}, u32[]{:S(2)}) %copy-start.1) | copy-done | bytes 10264
  2.9 0.0 copy-start.2
  2.9 0.7 %copy-done.2 = bf16[1,4,1280]{2,1,0:T(4,128)(2,1)S(1)} copy-done((bf16[1,4,1280]{2,1,0:T(4,128)(2,1)S(1)}, bf16[1,4,1280]{2,1,0:T(4,128)(2,1)}, u32[]{:S(2)}) %copy-start.2) | copy-done | bytes 10264
  3.6 0.0 copy-start.3
  3.6 0.7 %copy-done.3 = bf16[1,4,1280]{2,1,0:T(4,128)(2,1)S(1)} copy-done((bf16[1,4,1280]{2,1,0:T(4,128)(2,1)S(1)}, bf16[1,4,1280]{2,1,0:T(4,128)(2,1)}, u32[]{:S(2)}) %copy-start.3) | copy-done | bytes 10264
  4.3 57.0 %shard_map.76 = (bf16[96,1280]{1,0:T(8,128)(2,1)S(1)}, bf16[4,1280]{1,0:T(4,128)(2,1)S(1)}, f32[4,1280]{1,0:T(4,128)S(1)}) custom-call(bf16[768,1280]{1,0:T(8,128)(2,1)S(1)} %bitcast.8, bf16[4,1280]{1,0:T(4,128)(2,1)S(1)} %copy-done.1, bf16[4,1280]{1,0:T(4,128)(2,1)S(1)} %bitcast.9, bf16[4,1280]{1,0:T(4,128)(2,1)S(1)} %bitcast.10, bf16[768,1280]{1,0:T(8,128)(2,1)} %bitcast.11), custom_call_target="tpu_custom_call" | custom-call | flops 2000000000 | bytes 5000000 | tf_op jit(solution)/shard_map/pallas_call | solution.py:326
  61.3 0.7 %copy.11 = bf16[1,96,1280]{2,1,0:T(8,128)(2,1)} copy(bf16[1,96,1280]{2,1,0:T(8,128)(2,1)S(1)} %bitcast.6) | data formatting | bytes 491520
  62.0 0.6 copy.12
  62.6 0.6 copy.13
Async XLA Ops:
  0.6 1.5 %copy-start = (bf16[1,768,1280]{2,1,0:T(8,128)(2,1)S(1)}, bf16[1,768,1280]{2,1,0:T(8,128)(2,1)}, u32[]{:S(2)}) copy-start(bf16[1,768,1280]{2,1,0:T(8,128)(2,1)} %param.5) | copy-start | bytes 5898244
  2.2 0.7 %copy-start.1 = (bf16[4,1280]{1,0:T(4,128)(2,1)S(1)}, bf16[4,1280]{1,0:T(4,128)(2,1)}, u32[]{:S(2)}) copy-start(bf16[4,1280]{1,0:T(4,128)(2,1)} %phi_ref.1) | copy-start | bytes 30724
  2.9 0.7 %copy-start.2 = (bf16[1,4,1280]{2,1,0:T(4,128)(2,1)S(1)}, bf16[1,4,1280]{2,1,0:T(4,128)(2,1)}, u32[]{:S(2)}) copy-start(bf16[1,4,1280]{2,1,0:T(4,128)(2,1)} %param.7) | copy-start | bytes 30724
  3.6 0.7 %copy-start.3 = (bf16[1,4,1280]{2,1,0:T(4,128)(2,1)S(1)}, bf16[1,4,1280]{2,1,0:T(4,128)(2,1)}, u32[]{:S(2)}) copy-start(bf16[1,4,1280]{2,1,0:T(4,128)(2,1)} %param.8) | copy-start | bytes 30724

commit v2 on v1

--- a/solution.py
+++ b/solution.py
@@ -30,12 +30,12 @@
 
 
 def kernel(
-    tok_hbm, phi_ref, out_ref, inp_ref, og_hbm,
+    tok_hbm, phi_hbm, out_hbm, inp_hbm, og_hbm,
     tg_ref, so_ref, sw_ref,
     tok, og, shard, params, logit, cgrad, dgrad, row_exp, col_exp, col_tile, row_stat, col_stat,
     mat, comb, fac, part, stage, ring_in,
-    w_sum, o_sum, w_core, o_core, w_x, o_x, w_xin, o_xin, y_out, y_in, dp_out, dp_in,
-    load_sem, ys, yr, xs, xr, cs, cr, stat_s, stat_r, ring_s, ring_r, rc_s, rc_r, rx_s, rx_r, ry_s, ry_r, dp_s, dp_r,
+    w_sum, o_sum, w_core, o_core, w_mid, o_mid, w_min, o_min, w_end, o_end, w_ein, o_ein,
+    load_sem, ys, yr, xs, xr, cs, cr, stat_s, stat_r, ring_s, ring_r, rc_s, rc_r, rm_s, rm_r, re_s, re_r,
 ):
     dp = lax.axis_index("dp")
     seq = lax.axis_index("seq")
@@ -44,33 +44,41 @@
     x = lax.rem(seq // NC, NX)
     y = seq // (NC * NX)
 
-    def seq_of(yy, xx, cc):
-        return (yy * NX + xx) * NC + cc
-
+    a = jnp.where(core == 0, y, x)
+    b = jnp.where(core == 0, x, y)
+
+    def seq_of(aa, bb):
+        yy = jnp.where(core == 0, aa, bb)
+        xx = jnp.where(core == 0, bb, aa)
+        return (yy * NX + xx) * NC + core
+
+    barrier = pltpu.get_barrier_semaphore()
+
+    def greet(device):
+        pl.semaphore_signal(barrier, inc=1, device_id=device, device_id_type=MESH)
+
+    @pl.loop(1, NSEQ)
+    def _(j):
+        greet({"seq": lax.rem(seq + j, NSEQ)})
+
+    @pl.loop(1, NZ)
+    def _(j):
+        greet({"expert": lax.rem(z + j, NZ)})
+
+    for j in range(NY):
+        greet({"dp": 1 - dp, "seq": seq_of(lax.rem(a + j, NY), b)})
+
+    small = (phi_hbm, inp_hbm, out_hbm)
+    load_small = [
+        pltpu.make_async_copy(src, shard.at[a, t], load_sem.at[2 + t]) for t, src in enumerate(small)
+    ]
+    for copy in load_small:
+        copy.start()
     load_tok = pltpu.make_async_copy(tok_hbm, tok, load_sem.at[0])
     load_og = pltpu.make_async_copy(og_hbm, og, load_sem.at[1])
     load_tok.start()
     load_og.start()
-    shard[y, 0] = phi_ref[...]
-    shard[y, 1] = inp_ref[...]
-    shard[y, 2] = out_ref[...]
-
-    barrier = pltpu.get_barrier_semaphore()
-
-    @pl.loop(1, NSEQ)
-    def _(j):
-        pl.semaphore_signal(
-            barrier, inc=1, device_id={"seq": lax.rem(seq + j, NSEQ)}, device_id_type=MESH
-        )
-
-    @pl.loop(1, NZ)
-    def _(j):
-        pl.semaphore_signal(
-            barrier, inc=1, device_id={"expert": lax.rem(z + j, NZ)}, device_id_type=MESH
-        )
-
-    pl.semaphore_signal(barrier, inc=1, device_id={"dp": 1 - dp}, device_id_type=MESH)
-    pl.semaphore_wait(barrier, NSEQ + NZ - 1)
+    pl.semaphore_wait(barrier, NSEQ + NZ - 2 + NY)
 
     pending = []
 
@@ -84,30 +92,36 @@
         return copy
 
     y_copies = [
-        send(
-            shard.at[y], shard.at[y], ys.at[j - 1], yr.at[j - 1],
-            {"seq": seq_of(lax.rem(y + j, NY), x, core)},
-        )
+        [
+            send(
+                src, shard.at[a, t], ys.at[j - 1, t], yr.at[j - 1, t],
+                {"seq": seq_of(lax.rem(a + j, NY), b)},
+            )
+            for t, src in enumerate(small)
+        ]
         for j in range(1, NY)
     ]
-    for copy in y_copies:
-        copy.wait_recv()
+    for copy in load_small:
+        copy.wait()
+    for copies in y_copies:
+        for copy in copies:
+            copy.wait_recv()
     for t in range(3):
         rows = [shard[j, t].astype(F32) for j in range(NY)]
-        params[t, core, x] = jnp.concatenate(rows, axis=0).astype(BF16)
-    sibling = {"seq": seq_of(y, x, 1 - core)}
-    own_block = params.at[:, core, x]
+        params[t, core, b] = jnp.concatenate(rows, axis=0).astype(BF16)
+    sibling = {"seq": seq + 1 - 2 * core}
+    own_block = params.at[:, core, b]
     x_copies = [
         send(
             own_block, own_block, xs.at[j - 1], xr.at[j - 1],
-            {"seq": seq_of(y, lax.rem(x + j, NX), core)},
+            {"seq": seq_of(a, lax.rem(b + j, NX))},
         )
         for j in range(1, NX)
     ]
     c_copies = [send(own_block, own_block, cs.at[0], cr.at[0], sibling)]
     for j in (1, 3, 2):
         x_copies[j - 1].wait_recv()
-        block = params.at[:, core, lax.rem(x - j + NX, NX)]
+        block = params.at[:, core, lax.rem(b - j + NX, NX)]
         c_copies.append(send(block, block, cs.at[j], cr.at[j], sibling))
     load_tok.wait()
     load_og.wait()
@@ -144,19 +158,16 @@
         col_sum = jnp.sum(by_col, axis=1, keepdims=True)
         col_dot = jnp.sum(by_col * dgrad[rows, :], axis=1, keepdims=True)
         col_tile[rows, :] = jnp.where(
-            lane == 0, col_max, jnp.where(lane == 1, col_sum, jnp.where(lane == 2, col_dot, 0.0))
+            lane == 0,
+            col_max + jnp.log(col_sum),
+            jnp.where(lane == 1, col_dot / col_sum, jnp.where(lane == 2, col_max, 0.0)),
         )
-    row_stat[z] = jnp.concatenate(
-        [
-            row_max,
-            jnp.sum(row_sum, axis=0, keepdims=True),
-            jnp.sum(row_dot, axis=0, keepdims=True),
-            jnp.zeros((1, TOK), F32),
-        ],
-        axis=0,
-    )
-    col_stat[seq] = col_tile[...].T[0:4, :]
-
+    row_sum = jnp.sum(row_sum, axis=0, keepdims=True)
+    row_dot = jnp.sum(row_dot, axis=0, keepdims=True)
+    row_stat[z] = jnp.concatenate([row_max + jnp.log(row_sum), row_dot / row_sum], axis=0)
+    turned = col_tile[...].T
+    col_stat[seq] = turned[0:2, :]
+    col_top = turned[2:3, :]
     @pl.loop(1, NZ)
     def _(j):
         pltpu.make_async_remote_copy(
@@ -181,32 +192,32 @@
         best = stat[0][0:1]
         for j in range(1, count):
             best = jnp.maximum(best, stat[j][0:1])
-        total = jnp.zeros(stat.shape[1:], F32)
+        mass = jnp.zeros_like(best)
+        mean = jnp.zeros_like(best)
         for j in range(count):
             one = stat[j]
-            total = total + jnp.exp(one[0:1] - best) * one
-        return best, total[1:2], total[2:3]
-
-    best, mass, dot = join(row_stat, NZ)
-    row_scale = jnp.exp(row_stat[z][0:1] - best) / mass
-    row_mean = dot / mass
+            weight = jnp.exp(one[0:1] - best)
+            mass = mass + weight
+            mean = mean + weight * one[1:2]
+        return best, mass, mean / mass
+
+    best, mass, row_mean = join(row_stat, NZ)
+    row_scale = jnp.exp(row_max - best) / mass
     pltpu.make_async_copy(col_all, col_all, stat_r.at[1]).wait()
-    best, mass, dot = join(col_stat, NSEQ)
+    best, mass, col_mean = join(col_stat, NSEQ)
     lines = lax.broadcasted_iota(jnp.int32, (EXP, EXP), 0)
     col_tile[...] = jnp.where(
-        lines == 0,
-        jnp.exp(col_stat[seq][0:1] - best) / mass,
-        jnp.where(lines == 1, dot / mass, 0.0),
+        lines == 0, jnp.exp(col_top - best) / mass, jnp.where(lines == 1, col_mean, 0.0)
     ).T
 
-    for b, rows in enumerate(blocks):
+    for n, rows in enumerate(blocks):
         combine = row_exp[rows, :] * row_scale
         dispatch = col_exp[rows, :] * col_tile[rows, 0:1]
         grad = combine * (cgrad[rows, :] - row_mean) + dispatch * (dgrad[rows, :] - col_tile[rows, 1:2])
         high = grad.astype(BF16)
         mat[rows, :] = (grad - high.astype(F32)).astype(BF16)
-        mat[EXP + ROWS * b:EXP + ROWS * (b + 1), :] = high
-        mat[2 * EXP + ROWS * b:2 * EXP + ROWS * (b + 1), :] = dispatch.astype(BF16)
+        mat[EXP + ROWS * n:EXP + ROWS * (n + 1), :] = high
+        mat[2 * EXP + ROWS * n:2 * EXP + ROWS * (n + 1), :] = dispatch.astype(BF16)
         comb[rows, :] = combine.astype(BF16)
     fac[...] = mat[EXP:3 * EXP, :].T
 
@@ -256,54 +267,62 @@
 
     core_w.wait_recv()
     core_o.wait_recv()
-    w_x[...] = (w_sum[here, :] + w_core[...]).reshape(NX, 16, D)
-    o_x[...] = (o_sum[here, :].astype(F32) + o_core[...].astype(F32)).astype(BF16).reshape(NX, 16, D)
-    x_sums = []
+    w_mid[...] = (w_sum[here, :] + w_core[...]).reshape(NX, 16, D)
+    o_mid[...] = (o_sum[here, :].astype(F32) + o_core[...].astype(F32)).astype(BF16).reshape(NX, 16, D)
+    mid_sums = []
     for j in range(1, NX):
-        to = lax.rem(x + j, NX)
-        device = {"seq": seq_of(y, to, core)}
-        x_sums.append(send(w_x.at[to], w_xin.at[j - 1], rx_s.at[0, j - 1], rx_r.at[0, j - 1], device))
-        x_sums.append(send(o_x.at[to], o_xin.at[j - 1], rx_s.at[1, j - 1], rx_r.at[1, j - 1], device))
+        to = lax.rem(b + j, NX)
+        device = {"seq": seq_of(a, to)}
+        mid_sums.append(send(w_mid.at[to], w_min.at[j - 1], rm_s.at[0, j - 1], rm_r.at[0, j - 1], device))
+        mid_sums.append(send(o_mid.at[to], o_min.at[j - 1], rm_s.at[1, j - 1], rm_r.at[1, j - 1], device))
 
     pass_on(0, 3)
     pass_on(1, 3)
     pass_on(0, 4)
     pass_on(1, 4)
 
-    for copy in x_sums:
+    for copy in mid_sums:
         copy.wait_recv()
-    w16 = w_x[x]
-    o16 = o_x[x].astype(F32)
+    w16 = w_mid[b]
+    o16 = o_mid[b].astype(F32)
     for j in range(NX - 1):
-        w16 = w16 + w_xin[j]
-        o16 = o16 + o_xin[j].astype(F32)
+        w16 = w16 + w_min[j]
+        o16 = o16 + o_min[j].astype(F32)
     for j in range(NY):
-        y_out[j, 0:4] = w16[4 * j:4 * j + 4]
-        y_out[j, 4:8] = o16[4 * j:4 * j + 4]
-    y_sums = []
-    for j in range(1, NY):
-        to = lax.rem(y + j, NY)
-        y_sums.append(
-            send(y_out.at[to], y_in.at[j - 1], ry_s.at[j - 1], ry_r.at[j - 1], {"seq": seq_of(to, x, core)})
+        w_end[j] = w16[4 * j:4 * j + 4]
+        o_end[j] = o16[4 * j:4 * j + 4]
+    slot = dp * NY + a
+    w_ein[slot] = w_end[a]
+    end_w, end_o = [], []
+    for j in range(NY):
+        to = lax.rem(a + j, NY)
+        device = seq_of(to, b)
+        end_w.append(
+            send(w_end.at[to], w_ein.at[slot], re_s.at[0, j], re_r.at[0, j], {"dp": 1 - dp, "seq": device})
         )
+        if j > 0:
+            end_w.append(send(w_end.at[to], w_ein.at[slot], re_s.at[1, j], re_r.at[1, j], {"seq": device}))
+            end_o.append(send(o_end.at[to], o_ein.at[j - 1], re_s.at[2, j], re_r.at[2, j], {"seq": device}))
 
     pass_on(0, 5)
     pass_on(1, 5)
 
-    for copy in y_sums:
+    for copy in end_o:
         copy.wait_recv()
-    total = y_out[y]
+    total = o_end[a]
     for j in range(NY - 1):
-        total = total + y_in[j]
-    dp_out[...] = total
-    dp_copy = send(dp_out, dp_in, dp_s, dp_r, {"dp": 1 - dp})
-    so_ref[...] = total[4:8].astype(BF16)
+        total = total + o_ein[j]
+    so_ref[...] = total.astype(BF16)
 
     pass_on(0, 6)
     pass_on(1, 6)
 
-    dp_copy.wait_recv()
-    sw_ref[...] = dp_out[0:4] + dp_in[0:4]
+    for copy in end_w:
+        copy.wait_recv()
+    total = w_ein[0]
+    for j in range(1, 2 * NY):
+        total = total + w_ein[j]
+    sw_ref[...] = total
 
     for h in (1, 0):
         value = part[0, HALF * h:HALF * (h + 1), :]
@@ -319,18 +338,28 @@
     pltpu.make_async_copy(col_all, col_all, stat_s.at[1]).wait()
 
 
+def write_out(*refs):
+    sems = refs[-1]
+    copies = [pltpu.make_async_copy(refs[i], refs[3 + i], sems.at[i]) for i in range(3)]
+    for copy in copies:
+        copy.start()
+    for copy in copies:
+        copy.wait()
+
+
 def on_device(tokens, slot_weight, slot_output, slot_input_grad, output_grad):
     vmem = pl.BlockSpec(memory_space=pltpu.VMEM)
     hbm = pl.BlockSpec(memory_space=pl.ANY)
     dma = pltpu.SemaphoreType.DMA
-    token_grad, slot_output_grad, slot_weight_grad = pl.pallas_call(
+    shapes = (
+        jax.ShapeDtypeStruct((OWN, D), BF16),
+        jax.ShapeDtypeStruct((4, D), BF16),
+        jax.ShapeDtypeStruct((4, D), F32),
+    )
+    results = pl.pallas_call(
         kernel,
-        out_shape=(
-            jax.ShapeDtypeStruct((OWN, D), BF16),
-            jax.ShapeDtypeStruct((4, D), BF16),
-            jax.ShapeDtypeStruct((4, D), F32),
-        ),
-        in_specs=[hbm, vmem, vmem, vmem, hbm],
+        out_shape=shapes,
+        in_specs=[hbm, hbm, hbm, hbm, hbm],
         out_specs=(vmem, vmem, vmem),
         scratch_shapes=[
             pltpu.VMEM((TOK, D), BF16),
@@ -343,8 +372,8 @@
             pltpu.VMEM((EXP, TOK), F32),
             pltpu.VMEM((EXP, TOK), F32),
             pltpu.VMEM((EXP, EXP), F32),
-            pltpu.VMEM((NZ, 4, TOK), F32),
-            pltpu.VMEM((NSEQ, 4, EXP), F32),
+            pltpu.VMEM((NZ, 2, TOK), F32),
+            pltpu.VMEM((NSEQ, 2, EXP), F32),
             pltpu.VMEM((3 * EXP, TOK), BF16),
             pltpu.VMEM((EXP, TOK), BF16),
             pltpu.VMEM((TOK, 2 * EXP), BF16),
@@ -359,28 +388,34 @@
             pltpu.VMEM((NX, 16, D), BF16),
             pltpu.VMEM((NX - 1, 16, D), F32),
             pltpu.VMEM((NX - 1, 16, D), BF16),
-            pltpu.VMEM((NY, 8, D), F32),
-            pltpu.VMEM((NY - 1, 8, D), F32),
-            pltpu.VMEM((8, D), F32),
-            pltpu.VMEM((8, D), F32),
-            dma((2,)),
-            dma((3,)), dma((3,)),
+            pltpu.VMEM((NY, 4, D), F32),
+            pltpu.VMEM((NY, 4, D), F32),
+            pltpu.VMEM((2 * NY, 4, D), F32),
+            pltpu.VMEM((NY - 1, 4, D), F32),
+            dma((5,)),
+            dma((3, 3)), dma((3, 3)),
             dma((3,)), dma((3,)),
             dma((4,)), dma((4,)),
             dma((2,)), dma((2,)),
             dma((2, 7)), dma((2, 7)),
             dma((2,)), dma((2,)),
             dma((2, 3)), dma((2, 3)),
-            dma((3,)), dma((3,)),
-            dma(()), dma(()),
+            dma((3, 4)), dma((3, 4)),
         ],
         compiler_params=pltpu.CompilerParams(
-            collective_id=0, has_side_effects=True, vmem_limit_bytes=50 * 1024 * 1024
+            collective_id=0, has_side_effects=True, vmem_limit_bytes=60 * 1024 * 1024
         ),
         cost_estimate=pl.CostEstimate(
             flops=2_000_000_000, bytes_accessed=5_000_000, transcendentals=250_000
         ),
     )(tokens[0], slot_weight, slot_output[0], slot_input_grad[0], output_grad[0])
+    token_grad, slot_output_grad, slot_weight_grad = pl.pallas_call(
+        write_out,
+        out_shape=shapes,
+        in_specs=[hbm] * 3,
+        out_specs=(hbm,) * 3,
+        scratch_shapes=[dma((3,))],
+    )(*results)
     return (token_grad[None], slot_output_grad[None], slot_weight_grad)
 
 

time: 64.1 us -> 67.6 us (1.055)
  the two profiles are of different devices: /device:TPU:6 before, /device:TPU:8 now
where the time goes in v2:
time: 67.6 us; the launch traced here: 67.5 us
  Pallas kernels  66.8 us (99%)
    pallas_call x1, Pallas kernels, on_device(): pl.pallas_call(kernel, out_shape=shapes, in_specs=[hbm, hbm, hbm, hbm, hb...  57.3 us
    pallas_call x1, Pallas kernels, on_device(): pl.pallas_call(write_out, out_shape=shapes, in_specs=[hbm] * 3, out_specs...  9.51 us

profile of v2, /device:TPU:8, one launch (start us, length us, event | category | flops | bytes accessed | tf_op | source)
XLA Modules:
  0.0 67.5 jit_solution(9414610849937085953)
XLA Ops:
  0.6 57.3 %shard_map.76 = (bf16[96,1280]{1,0:T(8,128)(2,1)}, bf16[4,1280]{1,0:T(4,128)(2,1)}, f32[4,1280]{1,0:T(4,128)}) custom-call(bf16[768,1280]{1,0:T(8,128)(2,1)} %bitcast.6, bf16[4,1280]{1,0:T(4,128)(2,1)} %phi_hbm.1, bf16[4,1280]{1,0:T(4,128)(2,1)} %bitcast.9, bf16[4,1280]{1,0:T(4,128)(2,1)} %bitcast.10, bf16[768,1280]{1,0:T(8,128)(2,1)} %bitcast.7), custom_call_target="tpu_custom_call" | custom-call | flops 2000000000 | bytes 5000000 | tf_op jit(solution)/shard_map/pallas_call | solution.py:359
  58.0 9.5 %shard_map.77 = (bf16[96,1280]{1,0:T(8,128)(2,1)}, bf16[4,1280]{1,0:T(4,128)(2,1)}, f32[4,1280]{1,0:T(4,128)}) custom-call(bf16[96,1280]{1,0:T(8,128)(2,1)} %get-tuple-element.9.refs_0_, bf16[4,1280]{1,0:T(4,128)(2,1)} %get-tuple-element.10.refs_1_, f32[4,1280]{1,0:T(4,128)} %get-tuple-element.11.refs_2_), custom_call_target="tpu_custom_call" | custom-call | tf_op jit(solution)/shard_map/pallas_call | solution.py:412

commit v3 on v2

--- a/solution.py
+++ b/solution.py
@@ -30,9 +30,9 @@
 
 
 def kernel(
-    tok_hbm, phi_hbm, out_hbm, inp_hbm, og_hbm,
+    tok_hbm, own_ref, og_hbm,
     tg_ref, so_ref, sw_ref,
-    tok, og, shard, params, logit, cgrad, dgrad, row_exp, col_exp, col_tile, row_stat, col_stat,
+    tok, og, shard, shard_out, params, outs, logit, cgrad, dgrad, row_exp, col_exp, col_tile, row_stat, col_stat,
     mat, comb, fac, part, stage, ring_in,
     w_sum, o_sum, w_core, o_core, w_mid, o_mid, w_min, o_min, w_end, o_end, w_ein, o_ein,
     load_sem, ys, yr, xs, xr, cs, cr, stat_s, stat_r, ring_s, ring_r, rc_s, rc_r, rm_s, rm_r, re_s, re_r,
@@ -44,12 +44,7 @@
     x = lax.rem(seq // NC, NX)
     y = seq // (NC * NX)
 
-    a = jnp.where(core == 0, y, x)
-    b = jnp.where(core == 0, x, y)
-
-    def seq_of(aa, bb):
-        yy = jnp.where(core == 0, aa, bb)
-        xx = jnp.where(core == 0, bb, aa)
+    def seq_of(yy, xx):
         return (yy * NX + xx) * NC + core
 
     barrier = pltpu.get_barrier_semaphore()
@@ -66,14 +61,8 @@
         greet({"expert": lax.rem(z + j, NZ)})
 
     for j in range(NY):
-        greet({"dp": 1 - dp, "seq": seq_of(lax.rem(a + j, NY), b)})
-
-    small = (phi_hbm, inp_hbm, out_hbm)
-    load_small = [
-        pltpu.make_async_copy(src, shard.at[a, t], load_sem.at[2 + t]) for t, src in enumerate(small)
-    ]
-    for copy in load_small:
-        copy.start()
+        greet({"dp": 1 - dp, "seq": seq_of(lax.rem(y + j, NY), x)})
+
     load_tok = pltpu.make_async_copy(tok_hbm, tok, load_sem.at[0])
     load_og = pltpu.make_async_copy(og_hbm, og, load_sem.at[1])
     load_tok.start()
@@ -91,51 +80,66 @@
         pending.append(copy)
         return copy
 
-    y_copies = [
-        [
-            send(
-                src, shard.at[a, t], ys.at[j - 1, t], yr.at[j - 1, t],
-                {"seq": seq_of(lax.rem(a + j, NY), b)},
-            )
-            for t, src in enumerate(small)
-        ]
-        for j in range(1, NY)
+    pair_near, out_near, pair_far, out_far = [], [], [], []
+    for j in range(1, NX):
+        x_peer, y_peer = seq_of(y, lax.rem(x + j, NX)), seq_of(lax.rem(y + j, NY), x)
+        out_near.append(
+            send(own_ref.at[2], shard_out.at[x], xs.at[0, j - 1], xr.at[0, j - 1], {"seq": x_peer})
+        )
+        pair_near.append(
+            send(own_ref.at[pl.ds(0, 2)], shard.at[y], ys.at[0, j - 1], yr.at[0, j - 1], {"seq": y_peer})
+        )
+    shard_out[x] = own_ref[2]
+    shard[y] = own_ref[0:2]
+    sibling = {"seq": seq + 1 - 2 * core}
+    for copy in out_near:
+        copy.wait_recv()
+    rows = [shard_out[j].astype(F32) for j in range(NX)]
+    outs[core, y] = jnp.concatenate(rows, axis=0).astype(BF16)
+    own_out = outs.at[core, y]
+    for j in range(1, NY):
+        out_far.append(
+            send(own_out, own_out, ys.at[1, j - 1], yr.at[1, j - 1], {"seq": seq_of(lax.rem(y + j, NY), x)})
+        )
+    for copy in pair_near:
+        copy.wait_recv()
+    for t in range(2):
+        rows = [shard[j, t].astype(F32) for j in range(NY)]
+        params[t, core, x] = jnp.concatenate(rows, axis=0).astype(BF16)
+    own_pair = params.at[:, core, x]
+    for j in range(1, NX):
+        pair_far.append(
+            send(own_pair, own_pair, xs.at[1, j - 1], xr.at[1, j - 1], {"seq": seq_of(y, lax.rem(x + j, NX))})
+        )
+    c_copies = [
+        send(own_out, own_out, cs.at[1, 0], cr.at[1, 0], sibling),
+        send(own_pair, own_pair, cs.at[0, 0], cr.at[0, 0], sibling),
     ]
-    for copy in load_small:
-        copy.wait()
-    for copies in y_copies:
-        for copy in copies:
-            copy.wait_recv()
-    for t in range(3):
-        rows = [shard[j, t].astype(F32) for j in range(NY)]
-        params[t, core, b] = jnp.concatenate(rows, axis=0).astype(BF16)
-    sibling = {"seq": seq + 1 - 2 * core}
-    own_block = params.at[:, core, b]
-    x_copies = [
-        send(
-            own_block, own_block, xs.at[j - 1], xr.at[j - 1],
-            {"seq": seq_of(a, lax.rem(b + j, NX))},
-        )
-        for j in range(1, NX)
-    ]
-    c_copies = [send(own_block, own_block, cs.at[0], cr.at[0], sibling)]
     for j in (1, 3, 2):
-        x_copies[j - 1].wait_recv()
-        block = params.at[:, core, lax.rem(b - j + NX, NX)]
-        c_copies.append(send(block, block, cs.at[j], cr.at[j], sibling))
+        out_far[j - 1].wait_recv()
+        block = outs.at[core, lax.rem(y - j + NY, NY)]
+        c_copies.append(send(block, block, cs.at[1, j], cr.at[1, j], sibling))
+        pair_far[j - 1].wait_recv()
+        block = params.at[:, core, lax.rem(x - j + NX, NX)]
+        c_copies.append(send(block, block, cs.at[0, j], cr.at[0, j], sibling))
     load_tok.wait()
     load_og.wait()
     for copy in c_copies:
         copy.wait_recv()
 
-    both = params[0:2].reshape(2 * EXP, D)
-    outs = params[2].reshape(EXP, D)
+    both = params[...].reshape(2 * EXP, D)
+    slot_outs = outs[...].reshape(EXP, D)
     for n in range(TOK // 256):
         cols = slice(256 * n, 256 * (n + 1))
         pair = nt_dot(both, tok[cols, :])
         logit[:, cols] = pair[:EXP]
         dgrad[:, cols] = pair[EXP:]
-        cgrad[:, cols] = nt_dot(outs, og[cols, :])
+        swapped = nt_dot(slot_outs, og[cols, :])
+        for c in range(NC):
+            for yy in range(NY):
+                for xx in range(NX):
+                    put, get = (c * NX + xx) * 16 + 4 * yy, (c * NY + yy) * 16 + 4 * xx
+                    cgrad[put:put + 4, cols] = swapped[get:get + 4]
 
     ROWS = 16
     blocks = [slice(ROWS * b, ROWS * (b + 1)) for b in range(EXP // ROWS)]
@@ -222,7 +226,7 @@
     fac[...] = mat[EXP:3 * EXP, :].T
 
     def term(d):
-        stacked = params[0:2].reshape(2 * EXP, D)
+        stacked = params[...].reshape(2 * EXP, D)
         owner = lax.rem(z + d, NZ)
         part[d] = nn_dot(fac[pl.ds(pl.multiple_of(owner * OWN, OWN), OWN), :], stacked)
 
@@ -271,8 +275,8 @@
     o_mid[...] = (o_sum[here, :].astype(F32) + o_core[...].astype(F32)).astype(BF16).reshape(NX, 16, D)
     mid_sums = []
     for j in range(1, NX):
-        to = lax.rem(b + j, NX)
-        device = {"seq": seq_of(a, to)}
+        to = lax.rem(x + j, NX)
+        device = {"seq": seq_of(y, to)}
         mid_sums.append(send(w_mid.at[to], w_min.at[j - 1], rm_s.at[0, j - 1], rm_r.at[0, j - 1], device))
         mid_sums.append(send(o_mid.at[to], o_min.at[j - 1], rm_s.at[1, j - 1], rm_r.at[1, j - 1], device))
 
@@ -283,20 +287,20 @@
 
     for copy in mid_sums:
         copy.wait_recv()
-    w16 = w_mid[b]
-    o16 = o_mid[b].astype(F32)
+    w16 = w_mid[x]
+    o16 = o_mid[x].astype(F32)
     for j in range(NX - 1):
         w16 = w16 + w_min[j]
         o16 = o16 + o_min[j].astype(F32)
     for j in range(NY):
         w_end[j] = w16[4 * j:4 * j + 4]
         o_end[j] = o16[4 * j:4 * j + 4]
-    slot = dp * NY + a
-    w_ein[slot] = w_end[a]
+    slot = dp * NY + y
+    w_ein[slot] = w_end[y]
     end_w, end_o = [], []
     for j in range(NY):
-        to = lax.rem(a + j, NY)
-        device = seq_of(to, b)
+        to = lax.rem(y + j, NY)
+        device = seq_of(to, x)
         end_w.append(
             send(w_end.at[to], w_ein.at[slot], re_s.at[0, j], re_r.at[0, j], {"dp": 1 - dp, "seq": device})
         )
@@ -309,7 +313,7 @@
 
     for copy in end_o:
         copy.wait_recv()
-    total = o_end[a]
+    total = o_end[y]
     for j in range(NY - 1):
         total = total + o_ein[j]
     so_ref[...] = total.astype(BF16)
@@ -356,16 +360,19 @@
         jax.ShapeDtypeStruct((4, D), BF16),
         jax.ShapeDtypeStruct((4, D), F32),
     )
+    own = jnp.concatenate([slot_weight[None], slot_input_grad, slot_output])
     results = pl.pallas_call(
         kernel,
         out_shape=shapes,
-        in_specs=[hbm, hbm, hbm, hbm, hbm],
+        in_specs=[hbm, vmem, hbm],
         out_specs=(vmem, vmem, vmem),
         scratch_shapes=[
             pltpu.VMEM((TOK, D), BF16),
             pltpu.VMEM((TOK, D), BF16),
-            pltpu.VMEM((NY, 3, 4, D), BF16),
-            pltpu.VMEM((3, NC, NX, 16, D), BF16),
+            pltpu.VMEM((NY, 2, 4, D), BF16),
+            pltpu.VMEM((NX, 4, D), BF16),
+            pltpu.VMEM((2, NC, NX, 16, D), BF16),
+            pltpu.VMEM((NC, NY, 16, D), BF16),
             pltpu.VMEM((EXP, TOK), F32),
             pltpu.VMEM((EXP, TOK), F32),
             pltpu.VMEM((EXP, TOK), F32),
@@ -392,10 +399,10 @@
             pltpu.VMEM((NY, 4, D), F32),
             pltpu.VMEM((2 * NY, 4, D), F32),
             pltpu.VMEM((NY - 1, 4, D), F32),
-            dma((5,)),
-            dma((3, 3)), dma((3, 3)),
-            dma((3,)), dma((3,)),
-            dma((4,)), dma((4,)),
+            dma((2,)),
+            dma((2, 3)), dma((2, 3)),
+            dma((2, 3)), dma((2, 3)),
+            dma((2, 4)), dma((2, 4)),
             dma((2,)), dma((2,)),
             dma((2, 7)), dma((2, 7)),
             dma((2,)), dma((2,)),
@@ -403,16 +410,16 @@
             dma((3, 4)), dma((3, 4)),
         ],
         compiler_params=pltpu.CompilerParams(
-            collective_id=0, has_side_effects=True, vmem_limit_bytes=60 * 1024 * 1024
+            collective_id=0, has_side_effects=True, vmem_limit_bytes=62 * 1024 * 1024 + 512 * 1024
         ),
         cost_estimate=pl.CostEstimate(
             flops=2_000_000_000, bytes_accessed=5_000_000, transcendentals=250_000
         ),
-    )(tokens[0], slot_weight, slot_output[0], slot_input_grad[0], output_grad[0])
+    )(tokens[0], own, output_grad[0])
     token_grad, slot_output_grad, slot_weight_grad = pl.pallas_call(
         write_out,
         out_shape=shapes,
-        in_specs=[hbm] * 3,
+        in_specs=[vmem] * 3,
         out_specs=(hbm,) * 3,
         scratch_shapes=[dma((3,))],
     )(*results)

time: 67.6 us -> 60 us (0.89)
  the two profiles are of different devices: /device:TPU:8 before, /device:TPU:6 now
where the time goes in v3:
time: 60 us; the launch traced here: 59.5 us
  Pallas kernels  57.5 us (96%)
  other arithmetic  1.37 us (2%)
  between operations  0.64 us (1%)
    pallas_call x1, Pallas kernels, on_device(): pl.pallas_call(kernel, out_shape=shapes, in_specs=[hbm, vmem, hbm], out_s...  55.8 us
    pallas_call x1, Pallas kernels, on_device(): pl.pallas_call(write_out, out_shape=shapes, in_specs=[vmem] * 3, out_spec...  1.69 us
    concatenate x1, other arithmetic, on_device(): own = jnp.concatenate([slot_weight[None], slot_input_grad, slot_output])  1.37 us

profile of v3, /device:TPU:6, one launch (start us, length us, event | category | flops | bytes accessed | tf_op | source)
XLA Modules:
  0.0 59.5 jit_solution(8307625418851765904)
XLA Ops:
  0.6 1.4 %pad_maximum_fusion.own_ref = bf16[3,4,1280]{2,1,0:T(4,128)(2,1)} fusion(bf16[1,4,1280]{2,1,0:T(4,128)(2,1)} %param.7, bf16[1,4,1280]{2,1,0:T(4,128)(2,1)} %param.8, bf16[1,4,1280]{2,1,0:T(4,128)(2,1)} %bitcast.5), kind=kLoop, calls=%fused_computation | loop fusion | flops 30720 | bytes 61440 | tf_op jit(solution)/shard_map/concatenate | solution.py:363
  2.0 55.8 %shard_map.76 = (bf16[96,1280]{1,0:T(8,128)(2,1)}, bf16[4,1280]{1,0:T(4,128)(2,1)}, f32[4,1280]{1,0:T(4,128)}) custom-call(bf16[768,1280]{1,0:T(8,128)(2,1)} %bitcast.6, bf16[3,4,1280]{2,1,0:T(4,128)(2,1)} %pad_maximum_fusion.own_ref, bf16[768,1280]{1,0:T(8,128)(2,1)} %bitcast.7), custom_call_target="tpu_custom_call" | custom-call | flops 2000000000 | bytes 5000000 | tf_op jit(solution)/shard_map/pallas_call | solution.py:364
  57.8 1.7 %shard_map.77 = (bf16[96,1280]{1,0:T(8,128)(2,1)}, bf16[4,1280]{1,0:T(4,128)(2,1)}, f32[4,1280]{1,0:T(4,128)}) custom-call(bf16[96,1280]{1,0:T(8,128)(2,1)} %get-tuple-element.9.refs_0_, bf16[4,1280]{1,0:T(4,128)(2,1)} %get-tuple-element.10.refs_1_, f32[4,1280]{1,0:T(4,128)} %get-tuple-element.11.refs_2_), custom_call_target="tpu_custom_call" | custom-call | tf_op jit(solution)/shard_map/pallas_call | solution.py:419

commit v4 on v3

--- a/solution.py
+++ b/solution.py
@@ -30,9 +30,9 @@
 
 
 def kernel(
-    tok_hbm, own_ref, og_hbm,
+    tok_hbm, phi_hbm, out_hbm, inp_hbm, og_hbm,
     tg_ref, so_ref, sw_ref,
-    tok, og, shard, shard_out, params, outs, logit, cgrad, dgrad, row_exp, col_exp, col_tile, row_stat, col_stat,
+    tok, og, own, shard, shard_out, params, outs, logit, cgrad, dgrad, row_exp, col_exp, col_tile, row_stat, col_stat,
     mat, comb, fac, part, stage, ring_in,
     w_sum, o_sum, w_core, o_core, w_mid, o_mid, w_min, o_min, w_end, o_end, w_ein, o_ein,
     load_sem, ys, yr, xs, xr, cs, cr, stat_s, stat_r, ring_s, ring_r, rc_s, rc_r, rm_s, rm_r, re_s, re_r,
@@ -47,6 +47,12 @@
     def seq_of(yy, xx):
         return (yy * NX + xx) * NC + core
 
+    load_own = [
+        pltpu.make_async_copy(src, own.at[t], load_sem.at[2 + t])
+        for t, src in enumerate((phi_hbm, inp_hbm, out_hbm))
+    ]
+    for copy in load_own:
+        copy.start()
     barrier = pltpu.get_barrier_semaphore()
 
     def greet(device):
@@ -67,6 +73,8 @@
     load_og = pltpu.make_async_copy(og_hbm, og, load_sem.at[1])
     load_tok.start()
     load_og.start()
+    for copy in load_own:
+        copy.wait()
     pl.semaphore_wait(barrier, NSEQ + NZ - 2 + NY)
 
     pending = []
@@ -84,13 +92,13 @@
     for j in range(1, NX):
         x_peer, y_peer = seq_of(y, lax.rem(x + j, NX)), seq_of(lax.rem(y + j, NY), x)
         out_near.append(
-            send(own_ref.at[2], shard_out.at[x], xs.at[0, j - 1], xr.at[0, j - 1], {"seq": x_peer})
+            send(own.at[2], shard_out.at[x], xs.at[0, j - 1], xr.at[0, j - 1], {"seq": x_peer})
         )
         pair_near.append(
-            send(own_ref.at[pl.ds(0, 2)], shard.at[y], ys.at[0, j - 1], yr.at[0, j - 1], {"seq": y_peer})
-        )
-    shard_out[x] = own_ref[2]
-    shard[y] = own_ref[0:2]
+            send(own.at[pl.ds(0, 2)], shard.at[y], ys.at[0, j - 1], yr.at[0, j - 1], {"seq": y_peer})
+        )
+    shard_out[x] = own[2]
+    shard[y] = own[0:2]
     sibling = {"seq": seq + 1 - 2 * core}
     for copy in out_near:
         copy.wait_recv()
@@ -360,15 +368,15 @@
         jax.ShapeDtypeStruct((4, D), BF16),
         jax.ShapeDtypeStruct((4, D), F32),
     )
-    own = jnp.concatenate([slot_weight[None], slot_input_grad, slot_output])
     results = pl.pallas_call(
         kernel,
         out_shape=shapes,
-        in_specs=[hbm, vmem, hbm],
+        in_specs=[hbm] * 5,
         out_specs=(vmem, vmem, vmem),
         scratch_shapes=[
             pltpu.VMEM((TOK, D), BF16),
             pltpu.VMEM((TOK, D), BF16),
+            pltpu.VMEM((3, 4, D), BF16),
             pltpu.VMEM((NY, 2, 4, D), BF16),
             pltpu.VMEM((NX, 4, D), BF16),
             pltpu.VMEM((2, NC, NX, 16, D), BF16),
@@ -399,7 +407,7 @@
             pltpu.VMEM((NY, 4, D), F32),
             pltpu.VMEM((2 * NY, 4, D), F32),
             pltpu.VMEM((NY - 1, 4, D), F32),
-            dma((2,)),
+            dma((5,)),
             dma((2, 3)), dma((2, 3)),
             dma((2, 3)), dma((2, 3)),
             dma((2, 4)), dma((2, 4)),
@@ -415,7 +423,7 @@
         cost_estimate=pl.CostEstimate(
             flops=2_000_000_000, bytes_accessed=5_000_000, transcendentals=250_000
         ),
-    )(tokens[0], own, output_grad[0])
+    )(tokens[0], slot_weight, slot_output[0], slot_input_grad[0], output_grad[0])
     token_grad, slot_output_grad, slot_weight_grad = pl.pallas_call(
         write_out,
         out_shape=shapes,

time: 60 us -> 58.1 us (0.968)
  other arithmetic: 1.37 us -> 0 us
    concatenate x1 -> x0, other arithmetic: 1.37 us -> none  [on_device(): own = jnp.concatenate([slot_weight[None], slot_input_grad, slot_output])]
where the time goes in v4:
time: 58.1 us; the launch traced here: 57.9 us
  Pallas kernels  57.3 us (99%)
  between operations  0.64 us (1%)
    pallas_call x1, Pallas kernels, on_device(): pl.pallas_call(kernel, out_shape=shapes, in_specs=[hbm] * 5, out_specs=(v...  55.6 us
    pallas_call x1, Pallas kernels, on_device(): pl.pallas_call(write_out, out_shape=shapes, in_specs=[vmem] * 3, out_spec...  1.69 us

profile of v4, /device:TPU:6, one launch (start us, length us, event | category | flops | bytes accessed | tf_op | source)
XLA Modules:
  0.0 57.9 jit_solution(10304178497791816916)
XLA Ops:
  0.6 55.6 %shard_map.76 = (bf16[96,1280]{1,0:T(8,128)(2,1)}, bf16[4,1280]{1,0:T(4,128)(2,1)}, f32[4,1280]{1,0:T(4,128)}) custom-call(bf16[768,1280]{1,0:T(8,128)(2,1)} %bitcast.6, bf16[4,1280]{1,0:T(4,128)(2,1)} %phi_hbm.1, bf16[4,1280]{1,0:T(4,128)(2,1)} %bitcast.9, bf16[4,1280]{1,0:T(4,128)(2,1)} %bitcast.10, bf16[768,1280]{1,0:T(8,128)(2,1)} %bitcast.7), custom_call_target="tpu_custom_call" | custom-call | flops 2000000000 | bytes 5000000 | tf_op jit(solution)/shard_map/pallas_call | solution.py:371
  56.2 1.7 %shard_map.77 = (bf16[96,1280]{1,0:T(8,128)(2,1)}, bf16[4,1280]{1,0:T(4,128)(2,1)}, f32[4,1280]{1,0:T(4,128)}) custom-call(bf16[96,1280]{1,0:T(8,128)(2,1)} %get-tuple-element.9.refs_0_, bf16[4,1280]{1,0:T(4,128)(2,1)} %get-tuple-element.10.refs_1_, f32[4,1280]{1,0:T(4,128)} %get-tuple-element.11.refs_2_), custom_call_target="tpu_custom_call" | custom-call | tf_op jit(solution)/shard_map/pallas_call | solution.py:427

commit v5 on v4

--- a/solution.py
+++ b/solution.py
@@ -10,7 +10,7 @@
 MESH = pl.DeviceIdType.MESH
 
 NY, NX, NC, NZ = 4, 4, 2, 8
-NSEQ = NY * NX * NC
+CHIPS = NY * NX
 D = 1280
 TOK = 768
 EXP = 128
@@ -32,10 +32,10 @@
 def kernel(
     tok_hbm, phi_hbm, out_hbm, inp_hbm, og_hbm,
     tg_ref, so_ref, sw_ref,
-    tok, og, own, shard, shard_out, params, outs, logit, cgrad, dgrad, row_exp, col_exp, col_tile, row_stat, col_stat,
+    tok, og, own, shard, shard_out, params, outs, logit, cgrad, dgrad, row_exp, col_exp, col_tile, row_stat, col_stat, col_pair,
     mat, comb, fac, part, stage, ring_in,
     w_sum, o_sum, w_core, o_core, w_mid, o_mid, w_min, o_min, w_end, o_end, w_ein, o_ein,
-    load_sem, ys, yr, xs, xr, cs, cr, stat_s, stat_r, ring_s, ring_r, rc_s, rc_r, rm_s, rm_r, re_s, re_r,
+    load_sem, ys, yr, xs, xr, cs, cr, stat_s, stat_r, pair_s, pair_r, ring_s, ring_r, rc_s, rc_r, rm_s, rm_r, re_s, re_r,
 ):
     dp = lax.axis_index("dp")
     seq = lax.axis_index("seq")
@@ -58,9 +58,13 @@
     def greet(device):
         pl.semaphore_signal(barrier, inc=1, device_id=device, device_id_type=MESH)
 
-    @pl.loop(1, NSEQ)
+    chip = y * NX + x
+    sibling = {"seq": seq + 1 - 2 * core}
+    greet(sibling)
+
+    @pl.loop(1, CHIPS)
     def _(j):
-        greet({"seq": lax.rem(seq + j, NSEQ)})
+        greet({"seq": lax.rem(chip + j, CHIPS) * NC + core})
 
     @pl.loop(1, NZ)
     def _(j):
@@ -75,7 +79,7 @@
     load_og.start()
     for copy in load_own:
         copy.wait()
-    pl.semaphore_wait(barrier, NSEQ + NZ - 2 + NY)
+    pl.semaphore_wait(barrier, CHIPS + NZ - 1 + NY)
 
     pending = []
 
@@ -99,7 +103,6 @@
         )
     shard_out[x] = own[2]
     shard[y] = own[0:2]
-    sibling = {"seq": seq + 1 - 2 * core}
     for copy in out_near:
         copy.wait_recv()
     rows = [shard_out[j].astype(F32) for j in range(NX)]
@@ -178,8 +181,10 @@
     row_dot = jnp.sum(row_dot, axis=0, keepdims=True)
     row_stat[z] = jnp.concatenate([row_max + jnp.log(row_sum), row_dot / row_sum], axis=0)
     turned = col_tile[...].T
-    col_stat[seq] = turned[0:2, :]
+    col_pair[core] = turned[0:2, :]
     col_top = turned[2:3, :]
+    pair_copy = send(col_pair.at[core], col_pair.at[core], pair_s, pair_r, sibling)
+
     @pl.loop(1, NZ)
     def _(j):
         pltpu.make_async_remote_copy(
@@ -187,18 +192,6 @@
             send_sem=stat_s.at[0], recv_sem=stat_r.at[0],
             device_id={"expert": lax.rem(z + j, NZ)}, device_id_type=MESH,
         ).start()
-
-    @pl.loop(1, NSEQ)
-    def _(j):
-        pltpu.make_async_remote_copy(
-            src_ref=col_stat.at[seq], dst_ref=col_stat.at[seq],
-            send_sem=stat_s.at[1], recv_sem=stat_r.at[1],
-            device_id={"seq": lax.rem(seq + j, NSEQ)}, device_id_type=MESH,
-        ).start()
-
-    row_all = row_stat.at[pl.ds(0, NZ - 1)]
-    col_all = col_stat.at[pl.ds(0, NSEQ - 1)]
-    pltpu.make_async_copy(row_all, row_all, stat_r.at[0]).wait()
 
     def join(stat, count):
         best = stat[0][0:1]
@@ -213,10 +206,26 @@
             mean = mean + weight * one[1:2]
         return best, mass, mean / mass
 
+    pair_copy.wait_recv()
+    best, mass, col_mean = join(col_pair, NC)
+    col_stat[chip] = jnp.concatenate([best + jnp.log(mass), col_mean], axis=0)
+
+    @pl.loop(1, CHIPS)
+    def _(j):
+        pltpu.make_async_remote_copy(
+            src_ref=col_stat.at[chip], dst_ref=col_stat.at[chip],
+            send_sem=stat_s.at[1], recv_sem=stat_r.at[1],
+            device_id={"seq": lax.rem(chip + j, CHIPS) * NC + core}, device_id_type=MESH,
+        ).start()
+
+    row_all = row_stat.at[pl.ds(0, NZ - 1)]
+    col_all = col_stat.at[pl.ds(0, CHIPS - 1)]
+    pltpu.make_async_copy(row_all, row_all, stat_r.at[0]).wait()
+
     best, mass, row_mean = join(row_stat, NZ)
     row_scale = jnp.exp(row_max - best) / mass
     pltpu.make_async_copy(col_all, col_all, stat_r.at[1]).wait()
-    best, mass, col_mean = join(col_stat, NSEQ)
+    best, mass, col_mean = join(col_stat, CHIPS)
     lines = lax.broadcasted_iota(jnp.int32, (EXP, EXP), 0)
     col_tile[...] = jnp.where(
         lines == 0, jnp.exp(col_top - best) / mass, jnp.where(lines == 1, col_mean, 0.0)
@@ -292,6 +301,9 @@
     pass_on(1, 3)
     pass_on(0, 4)
     pass_on(1, 4)
+
+    pass_on(0, 5)
+    pass_on(1, 5)
 
     for copy in mid_sums:
         copy.wait_recv()
@@ -316,8 +328,8 @@
             end_w.append(send(w_end.at[to], w_ein.at[slot], re_s.at[1, j], re_r.at[1, j], {"seq": device}))
             end_o.append(send(o_end.at[to], o_ein.at[j - 1], re_s.at[2, j], re_r.at[2, j], {"seq": device}))
 
-    pass_on(0, 5)
-    pass_on(1, 5)
+    pass_on(0, 6)
+    pass_on(1, 6)
 
     for copy in end_o:
         copy.wait_recv()
@@ -325,9 +337,6 @@
     for j in range(NY - 1):
         total = total + o_ein[j]
     so_ref[...] = total.astype(BF16)
-
-    pass_on(0, 6)
-    pass_on(1, 6)
 
     for copy in end_w:
         copy.wait_recv()
@@ -370,7 +379,7 @@
     )
     results = pl.pallas_call(
         kernel,
-        out_shape=shapes,
+        out_shape=tuple(pltpu.VMEM(shape.shape, shape.dtype) for shape in shapes),
         in_specs=[hbm] * 5,
         out_specs=(vmem, vmem, vmem),
         scratch_shapes=[
@@ -388,7 +397,8 @@
             pltpu.VMEM((EXP, TOK), F32),
             pltpu.VMEM((EXP, EXP), F32),
             pltpu.VMEM((NZ, 2, TOK), F32),
-            pltpu.VMEM((NSEQ, 2, EXP), F32),
+            pltpu.VMEM((CHIPS, 2, EXP), F32),
+            pltpu.VMEM((NC, 2, EXP), F32),
             pltpu.VMEM((3 * EXP, TOK), BF16),
             pltpu.VMEM((EXP, TOK), BF16),
             pltpu.VMEM((TOK, 2 * EXP), BF16),
@@ -412,6 +422,7 @@
             dma((2, 3)), dma((2, 3)),
             dma((2, 4)), dma((2, 4)),
             dma((2,)), dma((2,)),
+            dma(()), dma(()),
             dma((2, 7)), dma((2, 7)),
             dma((2,)), dma((2,)),
             dma((2, 3)), dma((2, 3)),
@@ -430,7 +441,7 @@
         in_specs=[vmem] * 3,
         out_specs=(hbm,) * 3,
         scratch_shapes=[dma((3,))],
-    )(*results)
+    )(*[pltpu.with_memory_space_constraint(array, pltpu.VMEM) for array in results])
     return (token_grad[None], slot_output_grad[None], slot_weight_grad)
 
 

time: 58.1 us -> 55 us (0.947)
  Pallas kernels: 57.3 us -> 54.2 us
    pallas_call x1, Pallas kernels: 55.6 us -> 53.5 us  [on_device(): pl.pallas_call(kernel, out_shape=tuple((pltpu.VMEM(shape.shape, shape.dty...]
    pallas_call x1, Pallas kernels: 1.69 us -> 0.73 us  [on_device(): pl.pallas_call(write_out, out_shape=shapes, in_specs=[vmem] * 3, out_spec...]
where the time goes in v5:
time: 55 us; the launch traced here: 54.8 us
  Pallas kernels  54.2 us (99%)
  between operations  0.64 us (1%)
    pallas_call x1, Pallas kernels, on_device(): pl.pallas_call(kernel, out_shape=tuple((pltpu.VMEM(shape.shape, shape.dty...  53.5 us

profile of v5, /device:TPU:6, one launch (start us, length us, event | category | flops | bytes accessed | tf_op | source)
XLA Modules:
  0.0 54.8 jit_solution(1641293778983166132)
XLA Ops:
  0.6 53.5 %shard_map.76 = (bf16[96,1280]{1,0:T(8,128)(2,1)S(1)}, bf16[4,1280]{1,0:T(4,128)(2,1)S(1)}, f32[4,1280]{1,0:T(4,128)S(1)}) custom-call(bf16[768,1280]{1,0:T(8,128)(2,1)} %bitcast.6, bf16[4,1280]{1,0:T(4,128)(2,1)} %phi_hbm.1, bf16[4,1280]{1,0:T(4,128)(2,1)} %bitcast.9, bf16[4,1280]{1,0:T(4,128)(2,1)} %bitcast.10, bf16[768,1280]{1,0:T(8,128)(2,1)} %bitcast.7), custom_call_target="tpu_custom_call" | custom-call | flops 2000000000 | bytes 5000000 | tf_op jit(solution)/shard_map/pallas_call | solution.py:380
  54.1 0.7 %shard_map.77 = (bf16[96,1280]{1,0:T(8,128)(2,1)}, bf16[4,1280]{1,0:T(4,128)(2,1)}, f32[4,1280]{1,0:T(4,128)}) custom-call(bf16[96,1280]{1,0:T(8,128)(2,1)S(1)} %get-tuple-element.9.refs_0_, bf16[4,1280]{1,0:T(4,128)(2,1)S(1)} %get-tuple-element.10.refs_1_, f32[4,1280]{1,0:T(4,128)S(1)} %get-tuple-element.11.refs_2_), custom_call_target="tpu_custom_call" | custom-call | tf_op jit(solution)/shard_map/pallas_call | solution.py:438

commit v6 on v5

--- a/solution.py
+++ b/solution.py
@@ -16,6 +16,8 @@
 EXP = 128
 OWN = TOK // NZ
 HALF = OWN // 2
+PART = 48
+PARTS = HALF // PART
 
 RIGHT = ((4, 0), (3, 1), (3, 0), (2, 1), (2, 0), (1, 1), (1, 0))
 LEFT = ((4, 1), (3, 0), (3, 1), (2, 0), (2, 1), (1, 0), (1, 1))
@@ -154,19 +156,9 @@
 
     ROWS = 16
     blocks = [slice(ROWS * b, ROWS * (b + 1)) for b in range(EXP // ROWS)]
-    top = logit[blocks[0], :]
-    for rows in blocks[1:]:
-        top = jnp.maximum(top, logit[rows, :])
-    row_max = jnp.max(top, axis=0, keepdims=True)
-    row_sum = jnp.zeros((ROWS, TOK), F32)
-    row_dot = jnp.zeros((ROWS, TOK), F32)
     lane = lax.broadcasted_iota(jnp.int32, (ROWS, EXP), 1)
     for rows in blocks:
         value = logit[rows, :]
-        by_row = jnp.exp(value - row_max)
-        row_exp[rows, :] = by_row
-        row_sum = row_sum + by_row
-        row_dot = row_dot + by_row * cgrad[rows, :]
         col_max = jnp.max(value, axis=1, keepdims=True)
         by_col = jnp.exp(value - col_max)
         col_exp[rows, :] = by_col
@@ -177,13 +169,24 @@
             col_max + jnp.log(col_sum),
             jnp.where(lane == 1, col_dot / col_sum, jnp.where(lane == 2, col_max, 0.0)),
         )
-    row_sum = jnp.sum(row_sum, axis=0, keepdims=True)
-    row_dot = jnp.sum(row_dot, axis=0, keepdims=True)
-    row_stat[z] = jnp.concatenate([row_max + jnp.log(row_sum), row_dot / row_sum], axis=0)
     turned = col_tile[...].T
     col_pair[core] = turned[0:2, :]
     col_top = turned[2:3, :]
     pair_copy = send(col_pair.at[core], col_pair.at[core], pair_s, pair_r, sibling)
+    top = logit[blocks[0], :]
+    for rows in blocks[1:]:
+        top = jnp.maximum(top, logit[rows, :])
+    row_max = jnp.max(top, axis=0, keepdims=True)
+    row_sum = jnp.zeros((ROWS, TOK), F32)
+    row_dot = jnp.zeros((ROWS, TOK), F32)
+    for rows in blocks:
+        by_row = jnp.exp(logit[rows, :] - row_max)
+        row_exp[rows, :] = by_row
+        row_sum = row_sum + by_row
+        row_dot = row_dot + by_row * cgrad[rows, :]
+    row_sum = jnp.sum(row_sum, axis=0, keepdims=True)
+    row_dot = jnp.sum(row_dot, axis=0, keepdims=True)
+    row_stat[z] = jnp.concatenate([row_max + jnp.log(row_sum), row_dot / row_sum], axis=0)
 
     @pl.loop(1, NZ)
     def _(j):
@@ -252,16 +255,22 @@
 
     def pass_on(way, i):
         d, h = (RIGHT, LEFT)[way][i]
-        value = part[d if way == 0 else NZ - d, HALF * h:HALF * (h + 1), :]
-        if (d + 1, h) in ring[way]:
-            j, copy = ring[way][(d + 1, h)]
-            copy.wait_recv()
-            value = value + ring_in[way, j].astype(F32)
-        stage[way, i] = value.astype(BF16)
-        ring[way][(d, h)] = (
-            i,
-            send(stage.at[way, i], ring_in.at[way, i], ring_s.at[way, i], ring_r.at[way, i], towards[way]),
-        )
+        before = ring[way].get((d + 1, h))
+        copies = []
+        for q in range(PARTS):
+            first = HALF * h + PART * q
+            value = part[d if way == 0 else NZ - d, first:first + PART, :]
+            if before is not None:
+                before[1][q].wait_recv()
+                value = value + ring_in[way, before[0], q].astype(F32)
+            stage[way, i, q] = value.astype(BF16)
+            copies.append(
+                send(
+                    stage.at[way, i, q], ring_in.at[way, i, q], ring_s.at[way, i, q], ring_r.at[way, i, q],
+                    towards[way],
+                )
+            )
+        ring[way][(d, h)] = (i, copies)
 
     term(4)
     pass_on(0, 0)
@@ -346,12 +355,14 @@
     sw_ref[...] = total
 
     for h in (1, 0):
-        value = part[0, HALF * h:HALF * (h + 1), :]
-        for way in range(2):
-            j, copy = ring[way][(1, h)]
-            copy.wait_recv()
-            value = value + ring_in[way, j].astype(F32)
-        tg_ref[HALF * h:HALF * (h + 1), :] = value.astype(BF16)
+        for q in range(PARTS):
+            first = HALF * h + PART * q
+            value = part[0, first:first + PART, :]
+            for way in range(2):
+                i, copies = ring[way][(1, h)]
+                copies[q].wait_recv()
+                value = value + ring_in[way, i, q].astype(F32)
+            tg_ref[first:first + PART, :] = value.astype(BF16)
 
     for copy in pending:
         copy.wait_send()
@@ -403,8 +414,8 @@
             pltpu.VMEM((EXP, TOK), BF16),
             pltpu.VMEM((TOK, 2 * EXP), BF16),
             pltpu.VMEM((NZ, OWN, D), F32),
-            pltpu.VMEM((2, 7, HALF, D), BF16),
-            pltpu.VMEM((2, 7, HALF, D), BF16),
+            pltpu.VMEM((2, 7, PARTS, PART, D), BF16),
+            pltpu.VMEM((2, 7, PARTS, PART, D), BF16),
             pltpu.VMEM((EXP, D), F32),
             pltpu.VMEM((EXP, D), BF16),
             pltpu.VMEM((EXP // 2, D), F32),
@@ -423,7 +434,7 @@
             dma((2, 4)), dma((2, 4)),
             dma((2,)), dma((2,)),
             dma(()), dma(()),
-            dma((2, 7)), dma((2, 7)),
+            dma((2, 7, PARTS)), dma((2, 7, PARTS)),
             dma((2,)), dma((2,)),
             dma((2, 3)), dma((2, 3)),
             dma((3, 4)), dma((3, 4)),

time: 55 us -> 54.9 us (level)
  no operation moved by 1% of the time
where the time goes in v6:
time: 54.9 us; the launch traced here: 54.7 us
  Pallas kernels  54.1 us (99%)
  between operations  0.64 us (1%)
    pallas_call x1, Pallas kernels, on_device(): pl.pallas_call(kernel, out_shape=tuple((pltpu.VMEM(shape.shape, shape.dty...  53.3 us

profile of v6, /device:TPU:6, one launch (start us, length us, event | category | flops | bytes accessed | tf_op | source)
XLA Modules:
  0.0 54.7 jit_solution(6577714226717976711)
XLA Ops:
  0.6 53.3 %shard_map.76 = (bf16[96,1280]{1,0:T(8,128)(2,1)S(1)}, bf16[4,1280]{1,0:T(4,128)(2,1)S(1)}, f32[4,1280]{1,0:T(4,128)S(1)}) custom-call(bf16[768,1280]{1,0:T(8,128)(2,1)} %bitcast.6, bf16[4,1280]{1,0:T(4,128)(2,1)} %phi_hbm.1, bf16[4,1280]{1,0:T(4,128)(2,1)} %bitcast.9, bf16[4,1280]{1,0:T(4,128)(2,1)} %bitcast.10, bf16[768,1280]{1,0:T(8,128)(2,1)} %bitcast.7), custom_call_target="tpu_custom_call" | custom-call | flops 2000000000 | bytes 5000000 | tf_op jit(solution)/shard_map/pallas_call | solution.py:391
  54.0 0.7 %shard_map.77 = (bf16[96,1280]{1,0:T(8,128)(2,1)}, bf16[4,1280]{1,0:T(4,128)(2,1)}, f32[4,1280]{1,0:T(4,128)}) custom-call(bf16[96,1280]{1,0:T(8,128)(2,1)S(1)} %get-tuple-element.9.refs_0_, bf16[4,1280]{1,0:T(4,128)(2,1)S(1)} %get-tuple-element.10.refs_1_, f32[4,1280]{1,0:T(4,128)S(1)} %get-tuple-element.11.refs_2_), custom_call_target="tpu_custom_call" | custom-call | tf_op jit(solution)/shard_map/pallas_call | solution.py:449
